TPU v7x, 256 devices: a whole 4x4x8 slice. The times are simulated.
256 devices in a mesh: prow: 8 (over x, core), pcol: 32 (over y, z).
Axes of the slice: x: 4, y: 4, z: 8, core: 2. Of those that a mesh axis runs over, the one named last changes fastest.
Arguments:
- factor_blocks: float32 [6, 4, 8, 32, 256, 256], P(None, None, 'prow', 'pcol'), may hold values from -0.03125 to 0.03125
- block_pattern: int32 [6, 4, 8, 32], P(None, None, 'prow', 'pcol'), may hold values 0 or 1
- right_side: float32 [4, 32, 512, 256], P(None, 'pcol'), may hold values from -6 to 6
- diag_inverse: float32 [4, 32, 256, 256], P(None, 'pcol'), may hold values from -1 to 1.5, as said below
Outputs:
- forward_solution: float32 [4, 32, 512, 256], P(None, 'pcol')
- solution: float32 [4, 32, 512, 256], P(None, 'pcol', 'prow')
Inputs may be any that keep to these rules, and one draw needn't show every extreme that they name: Each block of diag_inverse is lower triangular with diagonal entries from 0.5 to 1.5.
All inputs are finite; a program needn't handle non-finite values. No bound on the sum of `block_pattern` on one device may be relied on, other than what follows from the above.
Results may differ from a plain program's by a relative error of at most 0.0001.
Values sent between devices are 32-bit elements; how exact they have to be, the bound alone decides.
No kernel may reach another device: no remote copies, remote signals or barrier semaphores. Data moves between devices by JAX's collectives and lax.ppermute only.
A program may use at most 64 MiB of HBM per device.

v0:
```python
import jax
import jax.numpy as jnp
from jax import lax
from jax.sharding import PartitionSpec as P

B = 256
NRHS = 512
LV = 4
SHARE = 64
HALF = 256
HIGH = lax.Precision.HIGH
HIGHEST = lax.Precision.HIGHEST

SHIFTED = (False, True, True, False)


def offset(shifted, low, half):
    return low * 0 if not shifted else half - low


def pair_number(later_level, earlier):
    return later_level * (later_level - 1) // 2 + earlier


def send(value, target):
    pairs = []
    for device in range(256):
        row, column = divmod(device, 32)
        there = target(row // 2, row % 2, column // 8, column // 2 % 4, column % 2)
        pairs.append((device, (there[0] * 2 + there[1]) * 32 + there[2] * 8 + there[3] * 2 + there[4]))
    return lax.ppermute(value, ("prow", "pcol"), pairs)


def to_y(value, k):
    return send(value, lambda x, c, y, h, l: (x, c, y ^ k, h, l))


def to_x(value, k):
    return send(value, lambda x, c, y, h, l: (x ^ k, c, y, h, l))


def to_core(value):
    return send(value, lambda x, c, y, h, l: (x, c ^ 1, y, h, l))


def to_pair(value, shifted):
    return send(value, lambda x, c, y, h, l: (x, c, y, (h - offset(shifted, l, l ^ 1)) % 4, l ^ 1))


def to_worker(value, shifted):
    return send(value, lambda x, c, y, h, l: (x, l, y, (h - offset(shifted, l, c)) % 4, c))


def from_worker(value, shifted):
    return send(value, lambda x, c, y, h, l: (x, l, y, (h + offset(shifted, c, l)) % 4, c))


def later(value, earlier):
    return value + 0.0 * earlier[(0,) * earlier.ndim]


def dot(left, right, left_axis, right_axis, precision=HIGH):
    return lax.dot_general(
        left,
        right,
        (((left_axis,), (right_axis,)), ((), ())),
        precision=precision,
        preferred_element_type=jnp.float32,
    )


def pick(value, index, axis):
    return lax.dynamic_index_in_dim(value, index, axis, keepdims=False)


def ordered(items, own):
    low, high = own % 2 == 1, own // 2 == 1
    pairs = [jnp.where(low, items[k ^ 1], items[k]) for k in range(4)]
    return jnp.concatenate([jnp.where(high, pairs[s ^ 2], pairs[s]) for s in range(4)])


def local(factor_blocks, block_pattern, right_side, diag_inverse):
    row = lax.axis_index("prow")
    column = lax.axis_index("pcol")
    x, core = row // 2, row % 2
    y, zh, zl = column // 8, column // 2 % 4, column % 2
    pattern = block_pattern[:, :, 0, 0].astype(jnp.float32)

    own_low = core == zl

    def by_half(own, other, axis):
        return jnp.concatenate([jnp.where(zl == 0, own, other), jnp.where(zl == 0, other, own)], axis)

    def by_column(mine, others):
        return jnp.where(own_low, mine, others), jnp.where(own_low, others, mine)

    def masked(number, earlier=()):
        weights = pattern[number]
        for item in earlier:
            weights = later(weights, item)
        return factor_blocks[number, :, 0, 0] * weights[:, None, None]

    own_blocks, other_blocks = {}, {}

    def exchange(number, earlier=()):
        shifted = SHIFTED[(0, 0, 1, 0, 1, 2)[number]]
        own_blocks[number] = masked(number, earlier)
        other_blocks[number] = to_pair(own_blocks[number], shifted)

    right = right_side[:, 0].reshape(LV, 8, SHARE, B)
    right_share, inverse = [None] * LV, [None] * LV

    def fetch(level, earlier=None):
        value = jnp.concatenate([diag_inverse[level, 0], pick(right[level], row, 0)])
        if earlier is not None:
            value = later(value, earlier)
        value = to_worker(value, SHIFTED[level])
        inverse[level], right_share[level] = value[:B], value[B:]

    exchange(0)
    exchange(2)
    fetch(1)
    exchange(1, (other_blocks[0],))
    exchange(4, (other_blocks[2],))
    fetch(2, other_blocks[1])
    fetch(3, other_blocks[1])
    fetch(0, other_blocks[1])
    before_z_stage = {1: (1, 4), 2: (3, 5), 3: ()}

    def update_to_share(parts, shifted, needed):
        moved = [to_y(parts(k), k) for k in (2, 1, 3)]
        total = parts(0)
        for value in moved:
            total = total + value
        for number in needed:
            total = later(total, other_blocks[number])
        total = total.reshape(4, SHARE, B)
        arrived = None
        for k in range(4):
            value = send(pick(total, zh ^ k, 0), lambda x, c, y, h, l: (h ^ k, c, y, (x - offset(shifted, c, l)) % 4, l))
            arrived = value if arrived is None else arrived + value
        return arrived

    def gather_rows(share):
        whole = ordered([share] + [to_x(share, k) for k in (1, 2, 3)], x)
        return by_column(whole, to_core(whole))

    def sum_rows(own, other):
        mine, others = by_column(own, other)
        total = (mine + to_core(others)).reshape(4, SHARE, B)
        moved = [to_x(pick(total, x ^ k, 0), k) for k in (2, 1, 3)]
        arrived = pick(total, x, 0)
        for value in moved:
            arrived = arrived + value
        return arrived

    def share_to_rows(share, shifted):
        items = []
        for k in range(4):
            items.append(send(share, lambda x, c, y, h, l: ((h + offset(shifted, c, l)) % 4, c, y, x ^ k, l)))
        whole = ordered(items, zh)
        moved = {k: to_y(whole, k) for k in (2, 1, 3)}
        return [whole, moved[1], moved[2], moved[3]]

    def block(number, k):
        return pick(own_blocks[number], y ^ k, 0), pick(other_blocks[number], y ^ k, 0)

    first = dot(right_side[0, 0], diag_inverse[0, 0], 1, 1, HIGHEST)
    halves = first.reshape(4, 2, SHARE, B)
    own_half = pick(halves, zl, 1).reshape(HALF, B)
    other_half = to_pair(pick(halves, 1 - zl, 1).reshape(HALF, B), SHIFTED[0])
    shares = [pick(jnp.where(own_low, own_half, other_half).reshape(4, SHARE, B), x, 0)]
    forward = [(own_half, other_half)]
    for current in range(1, LV):

        def parts(k):
            total = None
            for earlier in range(current):
                for value, factor in zip(forward[earlier], block(pair_number(current, earlier), k)):
                    term = dot(value, factor, 1, 1)
                    total = term if total is None else total + term
            return total

        arrived = update_to_share(parts, SHIFTED[current], before_z_stage[current])
        if current == 1:
            exchange(3, (arrived,))
            exchange(5, (arrived,))
        share = dot(right_share[current] - arrived, inverse[current], 1, 1, HIGHEST)
        shares.append(share)
        own, other = gather_rows(share)
        forward.append((own, other))

    def whole_forward(level, other):
        own = forward[level][0].reshape(4, 1, SHARE, B)
        return by_half(own, other.reshape(4, 1, SHARE, B), 1).reshape(NRHS, B)

    forward_out = [first] + [None] * (LV - 1)
    solution = [None] * LV
    rows_of = [None] * LV
    for current in range(LV - 1, -1, -1):
        update = shares[current]
        if current < LV - 1:
            partial_sums = [None, None]
            for later_level in range(LV - 1, current, -1):
                for k in range(4):
                    for side, factor in enumerate(block(pair_number(later_level, current), k)):
                        term = dot(rows_of[later_level][k], factor, 1, 0)
                        partial_sums[side] = term if partial_sums[side] is None else partial_sums[side] + term
            update = update - sum_rows(*partial_sums)
            update = later(later(update, solution[current + 1]), forward_other)
        solved = dot(update, inverse[current], 1, 0, HIGHEST)
        solution[current] = from_worker(solved, SHIFTED[current])
        if current > 0:
            forward_other = to_pair(later(forward[current][1], solved), SHIFTED[current])
            forward_out[current] = whole_forward(current, forward_other)
            rows_of[current] = share_to_rows(solved, SHIFTED[current])

    return jnp.stack(forward_out)[:, None], jnp.stack(solution)[:, None]


def solution(mesh):
    in_specs = (
        P(None, None, "prow", "pcol", None, None),
        P(None, None, "prow", "pcol"),
        P(None, "pcol", None, None),
        P(None, "pcol", None, None),
    )
    out_specs = (P(None, "pcol", None, None), P(None, "pcol", "prow", None))
    return jax.shard_map(local, mesh=mesh, in_specs=in_specs, out_specs=out_specs, check_vma=False)
```

profile of v0, /device:TPU:1, one launch (start us, length us, event | category | flops | bytes accessed | tf_op | source)
XLA Modules:
  0.0 398.0 jit_solution(17703078312259656530)
XLA Ops:
  2.9 6.5 %collective-permute-start.7 = (f32[4,256,256]{2,1,0:T(8,128)S(1)}, f32[4,256,256]{2,1,0:T(8,128)}, u32[]{:S(2)}, u32[]{:S(2)}) collective-permute-start(f32[4,256,256]{2,1,0:T(8,128)S(1)} %bitcast_multiply_fusion), channel_id=1, source_target_pairs={{0,7},{1,2},{2,1},{3,4},{4,3},{5,6},{6,5},{7,0},{8,15},{9,10},{10,... | collective-permute-start | bytes 3145736 | tf_op jit(solution)/shard_map/ppermute | solution.py:31
  25.9 6.5 %collective-permute-done.7 = f32[4,256,256]{2,1,0:T(8,128)} collective-permute-done((f32[4,256,256]{2,1,0:T(8,128)S(1)}, f32[4,256,256]{2,1,0:T(8,128)}, u32[]{:S(2)}, u32[]{:S(2)}) %collective-permute-start.7) | collective-permute-done | bytes 1048608 | tf_op jit(solution)/shard_map/ppermute | solution.py:31
  50.1 10.6 %collective-permute-done.6 = f32[4,256,256]{2,1,0:T(8,128)S(1)} collective-permute-done((f32[4,256,256]{2,1,0:T(8,128)S(1)}, f32[4,256,256]{2,1,0:T(8,128)S(1)}, u32[]{:S(2)}, u32[]{:S(2)}) %collective-permute-start.6) | collective-permute-done | bytes 1048608 | tf_op jit(solution)/shard_map/ppermute | solution.py:31
  60.6 7.2 %collective-permute-start = (f32[320,256]{1,0:T(8,128)S(1)}, f32[320,256]{1,0:T(8,128)S(1)}, u32[]{:S(2)}, u32[]{:S(2)}) collective-permute-start(f32[320,256]{1,0:T(8,128)S(1)} %copy-done.3), channel_id=1, source_target_pairs={{0,0},{1,34},{2,2},{3,36},{4,4},{5,38},{6,6},{7,32},{8,8},{9,42},{... | collective-permute-start | bytes 983048 | tf_op jit(solution)/shard_map/ppermute | solution.py:31
  71.7 3.6 collective-permute-start.12
  75.3 3.5 collective-permute-start.11
  80.8 5.7 %collective-permute-start.10 = (f32[64,256]{1,0:T(8,128)S(1)}, f32[64,256]{1,0:T(8,128)S(1)}, u32[]{:S(2)}, u32[]{:S(2)}) collective-permute-start(f32[64,256]{1,0:T(8,128)S(1)} %get-tuple-element.77), channel_id=1, source_target_pairs={{0,64},{1,71},{2,0},{3,7},{4,192},{5,199},{6,128},{7,135},{8,72},{... | collective-permute-start | bytes 196616 | tf_op jit(solution)/shard_map/ppermute | solution.py:31
  89.7 4.3 %collective-permute-start.13 = (f32[64,256]{1,0:T(8,128)S(1)}, f32[64,256]{1,0:T(8,128)S(1)}, u32[]{:S(2)}, u32[]{:S(2)}) collective-permute-start(f32[64,256]{1,0:T(8,128)S(1)} %fusion.238), channel_id=1, source_target_pairs={{0,192},{1,193},{2,194},{3,195},{4,196},{5,197},{6,198},{7,199},{8... | collective-permute-start | bytes 196616 | tf_op jit(solution)/shard_map/ppermute | solution.py:31
  102.7 5.6 %collective-permute-start.16 = (f32[256,256]{1,0:T(8,128)S(1)}, f32[256,256]{1,0:T(8,128)S(1)}, u32[]{:S(2)}, u32[]{:S(2)}) collective-permute-start(f32[256,256]{1,0:T(8,128)S(1)} %pad_maximum_fusion.4), channel_id=1, source_target_pairs={{0,32},{1,33},{2,34},{3,35},{4,36},{5,37},{6,38},{7,39},{8,40},{9,... | collective-permute-start | bytes 786440 | tf_op jit(solution)/shard_map/ppermute | solution.py:31
  123.3 11.4 %collective-permute-done.23 = f32[4,256,256]{2,1,0:T(8,128)S(1)} collective-permute-done((f32[4,256,256]{2,1,0:T(8,128)S(1)}, f32[4,256,256]{2,1,0:T(8,128)S(1)}, u32[]{:S(2)}, u32[]{:S(2)}) %collective-permute-start.23) | collective-permute-done | bytes 1048608 | tf_op jit(solution)/shard_map/ppermute | solution.py:31
  134.7 4.8 %collective-permute-start.19 = (f32[320,256]{1,0:T(8,128)S(1)}, f32[320,256]{1,0:T(8,128)S(1)}, u32[]{:S(2)}, u32[]{:S(2)}) collective-permute-start(f32[320,256]{1,0:T(8,128)S(1)} %maximum_add_fusion.1), channel_id=1, source_target_pairs={{0,0},{1,34},{2,2},{3,36},{4,4},{5,38},{6,6},{7,32},{8,8},{9,42},{... | collective-permute-start | bytes 983048 | tf_op jit(solution)/shard_map/ppermute | solution.py:31
  149.0 7.0 %collective-permute-start.25 = (f32[64,256]{1,0:T(8,128)S(1)}, f32[64,256]{1,0:T(8,128)S(1)}, u32[]{:S(2)}, u32[]{:S(2)}) collective-permute-start(f32[64,256]{1,0:T(8,128)S(1)} %get-tuple-element.69), channel_id=1, source_target_pairs={{0,64},{1,71},{2,0},{3,7},{4,192},{5,199},{6,128},{7,135},{8,72},{... | collective-permute-start | bytes 196616 | tf_op jit(solution)/shard_map/ppermute | solution.py:31
  156.4 6.6 %collective-permute-start.17 = (f32[320,256]{1,0:T(8,128)S(1)}, f32[320,256]{1,0:T(8,128)S(1)}, u32[]{:S(2)}, u32[]{:S(2)}) collective-permute-start(f32[320,256]{1,0:T(8,128)S(1)} %maximum_add_fusion), channel_id=1, source_target_pairs={{0,0},{1,32},{2,2},{3,34},{4,4},{5,36},{6,6},{7,38},{8,8},{9,40},{... | collective-permute-start | bytes 983048 | tf_op jit(solution)/shard_map/ppermute | solution.py:31
  165.1 10.2 %collective-permute-start.30 = (f32[64,256]{1,0:T(8,128)S(1)}, f32[64,256]{1,0:T(8,128)S(1)}, u32[]{:S(2)}, u32[]{:S(2)}) collective-permute-start(f32[64,256]{1,0:T(8,128)S(1)} %fusion.234), channel_id=1, source_target_pairs={{0,64},{1,65},{2,66},{3,67},{4,68},{5,69},{6,70},{7,71},{8,72},{9,... | collective-permute-start | bytes 196616 | tf_op jit(solution)/shard_map/ppermute | solution.py:31
  191.6 7.3 %collective-permute-done.32 = f32[256,256]{1,0:T(8,128)S(1)} collective-permute-done((f32[256,256]{1,0:T(8,128)S(1)}, f32[256,256]{1,0:T(8,128)S(1)}, u32[]{:S(2)}, u32[]{:S(2)}) %collective-permute-start.32) | collective-permute-done | bytes 262176 | tf_op jit(solution)/shard_map/ppermute | solution.py:31
  209.6 10.8 %collective-permute-done.36 = f32[64,256]{1,0:T(8,128)S(1)} collective-permute-done((f32[64,256]{1,0:T(8,128)S(1)}, f32[64,256]{1,0:T(8,128)S(1)}, u32[]{:S(2)}, u32[]{:S(2)}) %collective-permute-start.36) | collective-permute-done | bytes 65568 | tf_op jit(solution)/shard_map/ppermute | solution.py:31
  224.5 4.7 %collective-permute-start.40 = (f32[64,256]{1,0:T(8,128)S(1)}, f32[64,256]{1,0:T(8,128)S(1)}, u32[]{:S(2)}, u32[]{:S(2)}) collective-permute-start(f32[64,256]{1,0:T(8,128)S(1)} %fusion.228), channel_id=1, source_target_pairs={{0,4},{1,5},{2,68},{3,69},{4,132},{5,133},{6,196},{7,197},{8,12},{... | collective-permute-start | bytes 196616 | tf_op jit(solution)/shard_map/ppermute | solution.py:31
  230.6 6.3 %collective-permute-start.50 = (f32[64,256]{1,0:T(8,128)S(1)}, f32[64,256]{1,0:T(8,128)S(1)}, u32[]{:S(2)}, u32[]{:S(2)}) collective-permute-start(f32[64,256]{1,0:T(8,128)S(1)} %fusion.228), channel_id=1, source_target_pairs={{0,0},{1,32},{2,2},{3,34},{4,4},{5,36},{6,6},{7,38},{8,8},{9,40},{... | collective-permute-start | bytes 196616 | tf_op jit(solution)/shard_map/ppermute | solution.py:31
  237.5 3.6 collective-permute-start.82
  247.4 8.1 %collective-permute-done.45 = f32[256,256]{1,0:T(8,128)S(1)} collective-permute-done((f32[256,256]{1,0:T(8,128)S(1)}, f32[256,256]{1,0:T(8,128)S(1)}, u32[]{:S(2)}, u32[]{:S(2)}) %collective-permute-start.45) | collective-permute-done | bytes 262176 | tf_op jit(solution)/shard_map/ppermute | solution.py:31
  260.9 10.7 %collective-permute-start.49 = (f32[64,256]{1,0:T(8,128)S(1)}, f32[64,256]{1,0:T(8,128)S(1)}, u32[]{:S(2)}, u32[]{:S(2)}) collective-permute-start(f32[64,256]{1,0:T(8,128)S(1)} %get-tuple-element.51), channel_id=1, source_target_pairs={{0,192},{1,193},{2,194},{3,195},{4,196},{5,197},{6,198},{7,199},{8... | collective-permute-start | bytes 196616 | tf_op jit(solution)/shard_map/ppermute | solution.py:31
  279.1 5.1 %collective-permute-start.56 = (f32[64,256]{1,0:T(8,128)S(1)}, f32[64,256]{1,0:T(8,128)S(1)}, u32[]{:S(2)}, u32[]{:S(2)}) collective-permute-start(f32[64,256]{1,0:T(8,128)S(1)} %fusion.232), channel_id=1, source_target_pairs={{0,6},{1,71},{2,70},{3,135},{4,134},{5,199},{6,198},{7,7},{8,14},{... | collective-permute-start | bytes 196616 | tf_op jit(solution)/shard_map/ppermute | solution.py:31
  284.2 4.1 %collective-permute-start.57 = (f32[64,256]{1,0:T(8,128)S(1)}, f32[64,256]{1,0:T(8,128)S(1)}, u32[]{:S(2)}, u32[]{:S(2)}) collective-permute-start(f32[64,256]{1,0:T(8,128)S(1)} %fusion.232), channel_id=1, source_target_pairs={{0,4},{1,69},{2,68},{3,133},{4,132},{5,197},{6,196},{7,5},{8,12},{... | collective-permute-start | bytes 196616 | tf_op jit(solution)/shard_map/ppermute | solution.py:31
  290.2 4.5 %collective-permute-start.59 = (f32[64,256]{1,0:T(8,128)S(1)}, f32[64,256]{1,0:T(8,128)S(1)}, u32[]{:S(2)}, u32[]{:S(2)}) collective-permute-start(f32[64,256]{1,0:T(8,128)S(1)} %fusion.232), channel_id=1, source_target_pairs={{0,0},{1,65},{2,64},{3,129},{4,128},{5,193},{6,192},{7,1},{8,8},{9... | collective-permute-start | bytes 196616 | tf_op jit(solution)/shard_map/ppermute | solution.py:31
  295.4 3.6 collective-permute-start.67
  329.8 7.8 %collective-permute-start.70 = (f32[64,256]{1,0:T(8,128)S(1)}, f32[64,256]{1,0:T(8,128)S(1)}, u32[]{:S(2)}, u32[]{:S(2)}) collective-permute-start(f32[64,256]{1,0:T(8,128)S(1)} %fusion.236), channel_id=1, source_target_pairs={{0,6},{1,71},{2,70},{3,135},{4,134},{5,199},{6,198},{7,7},{8,14},{... | collective-permute-start | bytes 196616 | tf_op jit(solution)/shard_map/ppermute | solution.py:31
  339.2 4.3 %collective-permute-start.72 = (f32[64,256]{1,0:T(8,128)S(1)}, f32[64,256]{1,0:T(8,128)S(1)}, u32[]{:S(2)}, u32[]{:S(2)}) collective-permute-start(f32[64,256]{1,0:T(8,128)S(1)} %fusion.236), channel_id=1, source_target_pairs={{0,2},{1,67},{2,66},{3,131},{4,130},{5,195},{6,194},{7,3},{8,10},{... | collective-permute-start | bytes 196616 | tf_op jit(solution)/shard_map/ppermute | solution.py:31
  346.9 6.0 %collective-permute-start.81 = (f32[64,256]{1,0:T(8,128)S(1)}, f32[64,256]{1,0:T(8,128)S(1)}, u32[]{:S(2)}, u32[]{:S(2)}) collective-permute-start(f32[64,256]{1,0:T(8,128)S(1)} %fusion.236), channel_id=1, source_target_pairs={{0,0},{1,34},{2,2},{3,36},{4,4},{5,38},{6,6},{7,32},{8,8},{9,42},{... | collective-permute-start | bytes 196616 | tf_op jit(solution)/shard_map/ppermute | solution.py:31
  355.8 11.7 %collective-permute-done.76 = f32[256,256]{1,0:T(8,128)S(1)} collective-permute-done((f32[256,256]{1,0:T(8,128)S(1)}, f32[256,256]{1,0:T(8,128)S(1)}, u32[]{:S(2)}, u32[]{:S(2)}) %collective-permute-start.76) | collective-permute-done | bytes 262176 | tf_op jit(solution)/shard_map/ppermute | solution.py:31
  370.8 3.5 collective-permute-done.74
  381.2 3.7 collective-permute-start.78
  388.2 6.8 %collective-permute-start.83 = (f32[64,256]{1,0:T(8,128)S(1)}, f32[64,256]{1,0:T(8,128)S(1)}, u32[]{:S(2)}, u32[]{:S(2)}) collective-permute-start(f32[64,256]{1,0:T(8,128)S(1)} %fusion.66), channel_id=1, source_target_pairs={{0,0},{1,32},{2,2},{3,34},{4,4},{5,36},{6,6},{7,38},{8,8},{9,40},{... | collective-permute-start | bytes 196616 | tf_op jit(solution)/shard_map/ppermute | solution.py:31
  (319 shorter events, 178.5 us)
Async XLA Ops:
  2.9 29.5 %collective-permute-start.7 = (f32[4,256,256]{2,1,0:T(8,128)S(1)}, f32[4,256,256]{2,1,0:T(8,128)}, u32[]{:S(2)}, u32[]{:S(2)}) collective-permute-start(f32[4,256,256]{2,1,0:T(8,128)S(1)} %bitcast_multiply_fusion), channel_id=1, source_target_pairs={{0,7},{1,2},{2,1},{3,4},{4,3},{5,6},{6,5},{7,0},{8,15},{9,10},{10,... | collective-permute-start | bytes 3145736 | tf_op jit(solution)/shard_map/ppermute | solution.py:31
  10.8 23.9 %collective-permute-start.2 = (f32[4,256,256]{2,1,0:T(8,128)S(1)}, f32[4,256,256]{2,1,0:T(8,128)}, u32[]{:S(2)}, u32[]{:S(2)}) collective-permute-start(f32[4,256,256]{2,1,0:T(8,128)S(1)} %fusion.63), channel_id=1, source_target_pairs={{0,1},{1,0},{2,3},{3,2},{4,5},{5,4},{6,7},{7,6},{8,9},{9,8},{10,11... | collective-permute-start | bytes 3145736 | tf_op jit(solution)/shard_map/ppermute | solution.py:31
  13.4 26.8 %collective-permute-start.1 = (f32[256,256]{1,0:T(8,128)}, f32[256,256]{1,0:T(8,128)S(1)}, u32[]{:S(2)}, u32[]{:S(2)}) collective-permute-start(f32[256,256]{1,0:T(8,128)} %bitcast.11), channel_id=1, source_target_pairs={{0,1},{1,0},{2,3},{3,2},{4,5},{5,4},{6,7},{7,6},{8,9},{9,8},{10,11... | collective-permute-start | bytes 786440 | tf_op jit(solution)/shard_map/ppermute | solution.py:31
  38.5 22.2 %collective-permute-start.6 = (f32[4,256,256]{2,1,0:T(8,128)S(1)}, f32[4,256,256]{2,1,0:T(8,128)S(1)}, u32[]{:S(2)}, u32[]{:S(2)}) collective-permute-start(f32[4,256,256]{2,1,0:T(8,128)S(1)} %get-tuple-element.15), channel_id=1, source_target_pairs={{0,1},{1,0},{2,3},{3,2},{4,5},{5,4},{6,7},{7,6},{8,9},{9,8},{10,11... | collective-permute-start | bytes 3145736 | tf_op jit(solution)/shard_map/ppermute | solution.py:31
  41.5 28.9 %collective-permute-start.5 = (f32[256,256]{1,0:T(8,128)S(1)}, f32[256,256]{1,0:T(8,128)S(1)}, u32[]{:S(2)}, u32[]{:S(2)}) collective-permute-start(f32[256,256]{1,0:T(8,128)S(1)} %convolution_add_fusion.28), channel_id=1, source_target_pairs={{0,24},{1,25},{2,26},{3,27},{4,28},{5,29},{6,30},{7,31},{8,16},{9,... | collective-permute-start | bytes 786440 | tf_op jit(solution)/shard_map/ppermute | solution.py:31
  45.6 24.8 %collective-permute-start.4 = (f32[256,256]{1,0:T(8,128)S(1)}, f32[256,256]{1,0:T(8,128)S(1)}, u32[]{:S(2)}, u32[]{:S(2)}) collective-permute-start(f32[256,256]{1,0:T(8,128)S(1)} %convolution_add_fusion.29), channel_id=1, source_target_pairs={{0,8},{1,9},{2,10},{3,11},{4,12},{5,13},{6,14},{7,15},{8,0},{9,1},... | collective-permute-start | bytes 786440 | tf_op jit(solution)/shard_map/ppermute | solution.py:31
  45.7 23.5 %collective-permute-start.8 = (f32[4,256,256]{2,1,0:T(8,128)S(1)}, f32[4,256,256]{2,1,0:T(8,128)S(1)}, u32[]{:S(2)}, u32[]{:S(2)}) collective-permute-start(f32[4,256,256]{2,1,0:T(8,128)S(1)} %get-tuple-element.14), channel_id=1, source_target_pairs={{0,7},{1,2},{2,1},{3,4},{4,3},{5,6},{6,5},{7,0},{8,15},{9,10},{10,... | collective-permute-start | bytes 3145736 | tf_op jit(solution)/shard_map/ppermute | solution.py:31
  47.4 22.9 %collective-permute-start.3 = (f32[256,256]{1,0:T(8,128)S(1)}, f32[256,256]{1,0:T(8,128)S(1)}, u32[]{:S(2)}, u32[]{:S(2)}) collective-permute-start(f32[256,256]{1,0:T(8,128)S(1)} %convolution_add_fusion.30), channel_id=1, source_target_pairs={{0,16},{1,17},{2,18},{3,19},{4,20},{5,21},{6,22},{7,23},{8,24},{9,... | collective-permute-start | bytes 786440 | tf_op jit(solution)/shard_map/ppermute | solution.py:31
  60.6 28.7 %collective-permute-start = (f32[320,256]{1,0:T(8,128)S(1)}, f32[320,256]{1,0:T(8,128)S(1)}, u32[]{:S(2)}, u32[]{:S(2)}) collective-permute-start(f32[320,256]{1,0:T(8,128)S(1)} %copy-done.3), channel_id=1, source_target_pairs={{0,0},{1,34},{2,2},{3,36},{4,4},{5,38},{6,6},{7,32},{8,8},{9,42},{... | collective-permute-start | bytes 983048 | tf_op jit(solution)/shard_map/ppermute | solution.py:31
  71.7 16.4 %collective-permute-start.12 = (f32[64,256]{1,0:T(8,128)S(1)}, f32[64,256]{1,0:T(8,128)S(1)}, u32[]{:S(2)}, u32[]{:S(2)}) collective-permute-start(f32[64,256]{1,0:T(8,128)S(1)} %get-tuple-element.78), channel_id=1, source_target_pairs={{0,192},{1,199},{2,128},{3,135},{4,64},{5,71},{6,0},{7,7},{8,200},... | collective-permute-start | bytes 196616 | tf_op jit(solution)/shard_map/ppermute | solution.py:31
  98.7 42.1 %collective-permute-start.18 = (f32[4,256,256]{2,1,0:T(8,128)S(1)}, f32[4,256,256]{2,1,0:T(8,128)S(1)}, u32[]{:S(2)}, u32[]{:S(2)}) collective-permute-start(f32[4,256,256]{2,1,0:T(8,128)S(1)} %get-tuple-element.12), channel_id=1, source_target_pairs={{0,1},{1,0},{2,3},{3,2},{4,5},{5,4},{6,7},{7,6},{8,9},{9,8},{10,11... | collective-permute-start | bytes 3145736 | tf_op jit(solution)/shard_map/ppermute | solution.py:31
  108.7 26.1 %collective-permute-start.23 = (f32[4,256,256]{2,1,0:T(8,128)S(1)}, f32[4,256,256]{2,1,0:T(8,128)S(1)}, u32[]{:S(2)}, u32[]{:S(2)}) collective-permute-start(f32[4,256,256]{2,1,0:T(8,128)S(1)} %get-tuple-element.13), channel_id=1, source_target_pairs={{0,7},{1,2},{2,1},{3,4},{4,3},{5,6},{6,5},{7,0},{8,15},{9,10},{10,... | collective-permute-start | bytes 3145736 | tf_op jit(solution)/shard_map/ppermute | solution.py:31
  113.1 28.8 %collective-permute-start.22 = (f32[256,256]{1,0:T(8,128)S(1)}, f32[256,256]{1,0:T(8,128)S(1)}, u32[]{:S(2)}, u32[]{:S(2)}) collective-permute-start(f32[256,256]{1,0:T(8,128)S(1)} %fusion.12), channel_id=1, source_target_pairs={{0,24},{1,25},{2,26},{3,27},{4,28},{5,29},{6,30},{7,31},{8,16},{9,... | collective-permute-start | bytes 786440 | tf_op jit(solution)/shard_map/ppermute | solution.py:31
  114.9 27.0 %collective-permute-start.21 = (f32[256,256]{1,0:T(8,128)S(1)}, f32[256,256]{1,0:T(8,128)S(1)}, u32[]{:S(2)}, u32[]{:S(2)}) collective-permute-start(f32[256,256]{1,0:T(8,128)S(1)} %fusion.13), channel_id=1, source_target_pairs={{0,8},{1,9},{2,10},{3,11},{4,12},{5,13},{6,14},{7,15},{8,0},{9,1},... | collective-permute-start | bytes 786440 | tf_op jit(solution)/shard_map/ppermute | solution.py:31
  118.4 23.5 %collective-permute-start.20 = (f32[256,256]{1,0:T(8,128)S(1)}, f32[256,256]{1,0:T(8,128)S(1)}, u32[]{:S(2)}, u32[]{:S(2)}) collective-permute-start(f32[256,256]{1,0:T(8,128)S(1)} %fusion.14), channel_id=1, source_target_pairs={{0,16},{1,17},{2,18},{3,19},{4,20},{5,21},{6,22},{7,23},{8,24},{9,... | collective-permute-start | bytes 786440 | tf_op jit(solution)/shard_map/ppermute | solution.py:31
  134.7 21.6 %collective-permute-start.19 = (f32[320,256]{1,0:T(8,128)S(1)}, f32[320,256]{1,0:T(8,128)S(1)}, u32[]{:S(2)}, u32[]{:S(2)}) collective-permute-start(f32[320,256]{1,0:T(8,128)S(1)} %maximum_add_fusion.1), channel_id=1, source_target_pairs={{0,0},{1,34},{2,2},{3,36},{4,4},{5,38},{6,6},{7,32},{8,8},{9,42},{... | collective-permute-start | bytes 983048 | tf_op jit(solution)/shard_map/ppermute | solution.py:31
  142.4 20.6 %collective-permute-start.27 = (f32[64,256]{1,0:T(8,128)S(1)}, f32[64,256]{1,0:T(8,128)S(1)}, u32[]{:S(2)}, u32[]{:S(2)}) collective-permute-start(f32[64,256]{1,0:T(8,128)S(1)} %get-tuple-element.70), channel_id=1, source_target_pairs={{0,192},{1,199},{2,128},{3,135},{4,64},{5,71},{6,0},{7,7},{8,200},... | collective-permute-start | bytes 196616 | tf_op jit(solution)/shard_map/ppermute | solution.py:31
  145.1 17.9 %collective-permute-start.26 = (f32[64,256]{1,0:T(8,128)S(1)}, f32[64,256]{1,0:T(8,128)S(1)}, u32[]{:S(2)}, u32[]{:S(2)}) collective-permute-start(f32[64,256]{1,0:T(8,128)S(1)} %get-tuple-element.71), channel_id=1, source_target_pairs={{0,128},{1,135},{2,192},{3,199},{4,0},{5,7},{6,64},{7,71},{8,136},... | collective-permute-start | bytes 196616 | tf_op jit(solution)/shard_map/ppermute | solution.py:31
  146.8 16.2 %collective-permute-start.24 = (f32[64,256]{1,0:T(8,128)S(1)}, f32[64,256]{1,0:T(8,128)S(1)}, u32[]{:S(2)}, u32[]{:S(2)}) collective-permute-start(f32[64,256]{1,0:T(8,128)S(1)} %get-tuple-element.72), channel_id=1, source_target_pairs={{0,0},{1,7},{2,64},{3,71},{4,128},{5,135},{6,192},{7,199},{8,8},{9... | collective-permute-start | bytes 196616 | tf_op jit(solution)/shard_map/ppermute | solution.py:31
  156.4 51.3 %collective-permute-start.17 = (f32[320,256]{1,0:T(8,128)S(1)}, f32[320,256]{1,0:T(8,128)S(1)}, u32[]{:S(2)}, u32[]{:S(2)}) collective-permute-start(f32[320,256]{1,0:T(8,128)S(1)} %maximum_add_fusion), channel_id=1, source_target_pairs={{0,0},{1,32},{2,2},{3,34},{4,4},{5,36},{6,6},{7,38},{8,8},{9,40},{... | collective-permute-start | bytes 983048 | tf_op jit(solution)/shard_map/ppermute | solution.py:31
  205.3 15.2 %collective-permute-start.36 = (f32[64,256]{1,0:T(8,128)S(1)}, f32[64,256]{1,0:T(8,128)S(1)}, u32[]{:S(2)}, u32[]{:S(2)}) collective-permute-start(f32[64,256]{1,0:T(8,128)S(1)} %get-tuple-element.61), channel_id=1, source_target_pairs={{0,64},{1,65},{2,0},{3,1},{4,192},{5,193},{6,128},{7,129},{8,72},{... | collective-permute-start | bytes 196616 | tf_op jit(solution)/shard_map/ppermute | solution.py:31
  237.5 147.5 %collective-permute-start.82 = (f32[320,256]{1,0:T(8,128)S(1)}, f32[320,256]{1,0:T(8,128)S(1)}, u32[]{:S(2)}, u32[]{:S(2)}) collective-permute-start(f32[320,256]{1,0:T(8,128)S(1)} %maximum_add_fusion.2), channel_id=1, source_target_pairs={{0,0},{1,32},{2,2},{3,34},{4,4},{5,36},{6,6},{7,38},{8,8},{9,40},{... | collective-permute-start | bytes 983048 | tf_op jit(solution)/shard_map/ppermute | solution.py:31
  246.7 27.5 %collective-permute-start.55 = (f32[256,256]{1,0:T(8,128)S(1)}, f32[256,256]{1,0:T(8,128)S(1)}, u32[]{:S(2)}, u32[]{:S(2)}) collective-permute-start(f32[256,256]{1,0:T(8,128)S(1)} %select_add_fusion.2), channel_id=1, source_target_pairs={{0,1},{1,0},{2,3},{3,2},{4,5},{5,4},{6,7},{7,6},{8,9},{9,8},{10,11... | collective-permute-start | bytes 786440 | tf_op jit(solution)/shard_map/ppermute | solution.py:31
  260.9 14.5 %collective-permute-start.49 = (f32[64,256]{1,0:T(8,128)S(1)}, f32[64,256]{1,0:T(8,128)S(1)}, u32[]{:S(2)}, u32[]{:S(2)}) collective-permute-start(f32[64,256]{1,0:T(8,128)S(1)} %get-tuple-element.51), channel_id=1, source_target_pairs={{0,192},{1,193},{2,194},{3,195},{4,196},{5,197},{6,198},{7,199},{8... | collective-permute-start | bytes 196616 | tf_op jit(solution)/shard_map/ppermute | solution.py:31
  279.1 16.3 %collective-permute-start.56 = (f32[64,256]{1,0:T(8,128)S(1)}, f32[64,256]{1,0:T(8,128)S(1)}, u32[]{:S(2)}, u32[]{:S(2)}) collective-permute-start(f32[64,256]{1,0:T(8,128)S(1)} %fusion.232), channel_id=1, source_target_pairs={{0,6},{1,71},{2,70},{3,135},{4,134},{5,199},{6,198},{7,7},{8,14},{... | collective-permute-start | bytes 196616 | tf_op jit(solution)/shard_map/ppermute | solution.py:31
  284.2 14.8 %collective-permute-start.57 = (f32[64,256]{1,0:T(8,128)S(1)}, f32[64,256]{1,0:T(8,128)S(1)}, u32[]{:S(2)}, u32[]{:S(2)}) collective-permute-start(f32[64,256]{1,0:T(8,128)S(1)} %fusion.232), channel_id=1, source_target_pairs={{0,4},{1,69},{2,68},{3,133},{4,132},{5,197},{6,196},{7,5},{8,12},{... | collective-permute-start | bytes 196616 | tf_op jit(solution)/shard_map/ppermute | solution.py:31
  300.2 14.8 %collective-permute-start.61 = (f32[256,256]{1,0:T(8,128)S(1)}, f32[256,256]{1,0:T(8,128)S(1)}, u32[]{:S(2)}, u32[]{:S(2)}) collective-permute-start(f32[256,256]{1,0:T(8,128)S(1)} %pad_maximum_fusion.8), channel_id=1, source_target_pairs={{0,16},{1,17},{2,18},{3,19},{4,20},{5,21},{6,22},{7,23},{8,24},{9,... | collective-permute-start | bytes 786440 | tf_op jit(solution)/shard_map/ppermute | solution.py:31
  329.8 17.0 %collective-permute-start.70 = (f32[64,256]{1,0:T(8,128)S(1)}, f32[64,256]{1,0:T(8,128)S(1)}, u32[]{:S(2)}, u32[]{:S(2)}) collective-permute-start(f32[64,256]{1,0:T(8,128)S(1)} %fusion.236), channel_id=1, source_target_pairs={{0,6},{1,71},{2,70},{3,135},{4,134},{5,199},{6,198},{7,7},{8,14},{... | collective-permute-start | bytes 196616 | tf_op jit(solution)/shard_map/ppermute | solution.py:31
  337.6 15.2 %collective-permute-start.71 = (f32[64,256]{1,0:T(8,128)S(1)}, f32[64,256]{1,0:T(8,128)S(1)}, u32[]{:S(2)}, u32[]{:S(2)}) collective-permute-start(f32[64,256]{1,0:T(8,128)S(1)} %fusion.236), channel_id=1, source_target_pairs={{0,4},{1,69},{2,68},{3,133},{4,132},{5,197},{6,196},{7,5},{8,12},{... | collective-permute-start | bytes 196616 | tf_op jit(solution)/shard_map/ppermute | solution.py:31
  346.9 31.6 %collective-permute-start.81 = (f32[64,256]{1,0:T(8,128)S(1)}, f32[64,256]{1,0:T(8,128)S(1)}, u32[]{:S(2)}, u32[]{:S(2)}) collective-permute-start(f32[64,256]{1,0:T(8,128)S(1)} %fusion.236), channel_id=1, source_target_pairs={{0,0},{1,34},{2,2},{3,36},{4,4},{5,38},{6,6},{7,32},{8,8},{9,42},{... | collective-permute-start | bytes 196616 | tf_op jit(solution)/shard_map/ppermute | solution.py:31
  352.8 26.8 %collective-permute-start.69 = (f32[256,256]{1,0:T(8,128)S(1)}, f32[256,256]{1,0:T(8,128)S(1)}, u32[]{:S(2)}, u32[]{:S(2)}) collective-permute-start(f32[256,256]{1,0:T(8,128)S(1)} %broadcast_add_fusion), channel_id=1, source_target_pairs={{0,7},{1,2},{2,1},{3,4},{4,3},{5,6},{6,5},{7,0},{8,15},{9,10},{10,... | collective-permute-start | bytes 786440 | tf_op jit(solution)/shard_map/ppermute | solution.py:31
  353.8 15.4 %collective-permute-start.75 = (f32[256,256]{1,0:T(8,128)S(1)}, f32[256,256]{1,0:T(8,128)S(1)}, u32[]{:S(2)}, u32[]{:S(2)}) collective-permute-start(f32[256,256]{1,0:T(8,128)S(1)} %pad_maximum_fusion.9), channel_id=1, source_target_pairs={{0,16},{1,17},{2,18},{3,19},{4,20},{5,21},{6,22},{7,23},{8,24},{9,... | collective-permute-start | bytes 786440 | tf_op jit(solution)/shard_map/ppermute | solution.py:31
  (56 other events, 521.4 us)
where the time goes:
time: 404 us; the launch traced here: 398 us
  starting transfers between devices  209 us (52%)
  waiting for transfers between devices  94.8 us (23%)
  matrix products  49.8 us (12%)
  local copies, waits for them, and re-layouts  18.5 us (5%)
  between operations  13.1 us (3%)
  other arithmetic  12.3 us (3%)
    ppermute x84, starting transfers between devices, send(): return lax.ppermute(value, ('prow', 'pcol'), pairs)  209 us
    ppermute x84, waiting for transfers between devices, send(): return lax.ppermute(value, ('prow', 'pcol'), pairs)  94.8 us
    dot_general x104, matrix products, dot(): lax.dot_general(left, right, (((left_axis,), (right_axis,)), ((), ())), p...  49.8 us
    slice x16, local copies, waits for them, and re-layouts, later(): return value + 0.0 * earlier[(0,) * earlier.ndim]  9.55 us
  transfers between devices with their start and end apart: 84, of which 25 were waited for; matrix products, arithmetic and copies ran while one was open for 19% of the time, Pallas kernels for 0%

commit v1 on v0

--- a/solution.py
+++ b/solution.py
@@ -128,7 +128,7 @@
     before_z_stage = {1: (1, 4), 2: (3, 5), 3: ()}
 
     def update_to_share(parts, shifted, needed):
-        moved = [to_y(parts(k), k) for k in (2, 1, 3)]
+        moved = [to_y(parts(k), k) for k in (1, 3, 2)]
         total = parts(0)
         for value in moved:
             total = total + value
@@ -148,7 +148,7 @@
     def sum_rows(own, other):
         mine, others = by_column(own, other)
         total = (mine + to_core(others)).reshape(4, SHARE, B)
-        moved = [to_x(pick(total, x ^ k, 0), k) for k in (2, 1, 3)]
+        moved = [to_x(pick(total, x ^ k, 0), k) for k in (1, 3, 2)]
         arrived = pick(total, x, 0)
         for value in moved:
             arrived = arrived + value
@@ -159,7 +159,7 @@
         for k in range(4):
             items.append(send(share, lambda x, c, y, h, l: ((h + offset(shifted, c, l)) % 4, c, y, x ^ k, l)))
         whole = ordered(items, zh)
-        moved = {k: to_y(whole, k) for k in (2, 1, 3)}
+        moved = {k: to_y(whole, k) for k in (1, 3, 2)}
         return [whole, moved[1], moved[2], moved[3]]
 
     def block(number, k):
@@ -202,7 +202,7 @@
         if current < LV - 1:
             partial_sums = [None, None]
             for later_level in range(LV - 1, current, -1):
-                for k in range(4):
+                for k in (0, 1, 3, 2):
                     for side, factor in enumerate(block(pair_number(later_level, current), k)):
                         term = dot(rows_of[later_level][k], factor, 1, 0)
                         partial_sums[side] = term if partial_sums[side] is None else partial_sums[side] + term

time: 404 us -> 397 us (0.983)
  starting transfers between devices: 209 us -> 201 us
    ppermute x84, starting transfers between devices: 209 us -> 201 us  [send(): return lax.ppermute(value, ('prow', 'pcol'), pairs)]
  transfers between devices with their start and end apart: 84 -> 84, of which waited for: 25 -> 27; matrix products, arithmetic and copies ran while one was open for 19% -> 20% of each run, Pallas kernels for 0% -> 0%
where the time goes in v1:
time: 397 us; the launch traced here: 390 us
  starting transfers between devices  201 us (51%)
  waiting for transfers between devices  95.2 us (24%)
  matrix products  49.8 us (13%)
  local copies, waits for them, and re-layouts  18.5 us (5%)
  between operations  13.1 us (3%)
  other arithmetic  12.3 us (3%)
    ppermute x84, starting transfers between devices, send(): return lax.ppermute(value, ('prow', 'pcol'), pairs)  201 us
    ppermute x84, waiting for transfers between devices, send(): return lax.ppermute(value, ('prow', 'pcol'), pairs)  95.2 us
    dot_general x104, matrix products, dot(): lax.dot_general(left, right, (((left_axis,), (right_axis,)), ((), ())), p...  49.8 us
    slice x16, local copies, waits for them, and re-layouts, later(): return value + 0.0 * earlier[(0,) * earlier.ndim]  9.55 us
  transfers between devices with their start and end apart: 84, of which 27 were waited for; matrix products, arithmetic and copies ran while one was open for 20% of the time, Pallas kernels for 0%

profile of v1, /device:TPU:1, one launch (start us, length us, event | category | flops | bytes accessed | tf_op | source)
XLA Modules:
  0.0 390.2 jit_solution(13397661815007967095)
XLA Ops:
  2.9 6.5 %collective-permute-start.7 = (f32[4,256,256]{2,1,0:T(8,128)S(1)}, f32[4,256,256]{2,1,0:T(8,128)}, u32[]{:S(2)}, u32[]{:S(2)}) collective-permute-start(f32[4,256,256]{2,1,0:T(8,128)S(1)} %bitcast_multiply_fusion), channel_id=1, source_target_pairs={{0,7},{1,2},{2,1},{3,4},{4,3},{5,6},{6,5},{7,0},{8,15},{9,10},{10,... | collective-permute-start | bytes 3145736 | tf_op jit(solution)/shard_map/ppermute | solution.py:31
  25.9 6.5 %collective-permute-done.7 = f32[4,256,256]{2,1,0:T(8,128)} collective-permute-done((f32[4,256,256]{2,1,0:T(8,128)S(1)}, f32[4,256,256]{2,1,0:T(8,128)}, u32[]{:S(2)}, u32[]{:S(2)}) %collective-permute-start.7) | collective-permute-done | bytes 1048608 | tf_op jit(solution)/shard_map/ppermute | solution.py:31
  49.8 10.8 %collective-permute-done.6 = f32[4,256,256]{2,1,0:T(8,128)S(1)} collective-permute-done((f32[4,256,256]{2,1,0:T(8,128)S(1)}, f32[4,256,256]{2,1,0:T(8,128)S(1)}, u32[]{:S(2)}, u32[]{:S(2)}) %collective-permute-start.6) | collective-permute-done | bytes 1048608 | tf_op jit(solution)/shard_map/ppermute | solution.py:31
  60.6 7.2 %collective-permute-start = (f32[320,256]{1,0:T(8,128)S(1)}, f32[320,256]{1,0:T(8,128)S(1)}, u32[]{:S(2)}, u32[]{:S(2)}) collective-permute-start(f32[320,256]{1,0:T(8,128)S(1)} %copy-done.3), channel_id=1, source_target_pairs={{0,0},{1,34},{2,2},{3,36},{4,4},{5,38},{6,6},{7,32},{8,8},{9,42},{... | collective-permute-start | bytes 983048 | tf_op jit(solution)/shard_map/ppermute | solution.py:31
  75.3 4.1 %collective-permute-start.11 = (f32[64,256]{1,0:T(8,128)S(1)}, f32[64,256]{1,0:T(8,128)S(1)}, u32[]{:S(2)}, u32[]{:S(2)}) collective-permute-start(f32[64,256]{1,0:T(8,128)S(1)} %get-tuple-element.79), channel_id=1, source_target_pairs={{0,128},{1,135},{2,192},{3,199},{4,0},{5,7},{6,64},{7,71},{8,136},... | collective-permute-start | bytes 196616 | tf_op jit(solution)/shard_map/ppermute | solution.py:31
  81.4 5.7 %collective-permute-start.10 = (f32[64,256]{1,0:T(8,128)S(1)}, f32[64,256]{1,0:T(8,128)S(1)}, u32[]{:S(2)}, u32[]{:S(2)}) collective-permute-start(f32[64,256]{1,0:T(8,128)S(1)} %get-tuple-element.77), channel_id=1, source_target_pairs={{0,64},{1,71},{2,0},{3,7},{4,192},{5,199},{6,128},{7,135},{8,72},{... | collective-permute-start | bytes 196616 | tf_op jit(solution)/shard_map/ppermute | solution.py:31
  90.2 3.6 collective-permute-start.13
  98.6 3.6 collective-permute-start.18
  103.1 7.1 %collective-permute-start.16 = (f32[256,256]{1,0:T(8,128)S(1)}, f32[256,256]{1,0:T(8,128)S(1)}, u32[]{:S(2)}, u32[]{:S(2)}) collective-permute-start(f32[256,256]{1,0:T(8,128)S(1)} %pad_maximum_fusion.4), channel_id=1, source_target_pairs={{0,32},{1,33},{2,34},{3,35},{4,36},{5,37},{6,38},{7,39},{8,40},{9,... | collective-permute-start | bytes 786440 | tf_op jit(solution)/shard_map/ppermute | solution.py:31
  123.8 12.8 %collective-permute-done.23 = f32[4,256,256]{2,1,0:T(8,128)S(1)} collective-permute-done((f32[4,256,256]{2,1,0:T(8,128)S(1)}, f32[4,256,256]{2,1,0:T(8,128)S(1)}, u32[]{:S(2)}, u32[]{:S(2)}) %collective-permute-start.23) | collective-permute-done | bytes 1048608 | tf_op jit(solution)/shard_map/ppermute | solution.py:31
  136.6 4.7 %collective-permute-start.19 = (f32[320,256]{1,0:T(8,128)S(1)}, f32[320,256]{1,0:T(8,128)S(1)}, u32[]{:S(2)}, u32[]{:S(2)}) collective-permute-start(f32[320,256]{1,0:T(8,128)S(1)} %maximum_add_fusion.1), channel_id=1, source_target_pairs={{0,0},{1,34},{2,2},{3,36},{4,4},{5,38},{6,6},{7,32},{8,8},{9,42},{... | collective-permute-start | bytes 983048 | tf_op jit(solution)/shard_map/ppermute | solution.py:31
  150.7 7.0 %collective-permute-start.25 = (f32[64,256]{1,0:T(8,128)S(1)}, f32[64,256]{1,0:T(8,128)S(1)}, u32[]{:S(2)}, u32[]{:S(2)}) collective-permute-start(f32[64,256]{1,0:T(8,128)S(1)} %get-tuple-element.69), channel_id=1, source_target_pairs={{0,64},{1,71},{2,0},{3,7},{4,192},{5,199},{6,128},{7,135},{8,72},{... | collective-permute-start | bytes 196616 | tf_op jit(solution)/shard_map/ppermute | solution.py:31
  158.0 6.7 %collective-permute-start.17 = (f32[320,256]{1,0:T(8,128)S(1)}, f32[320,256]{1,0:T(8,128)S(1)}, u32[]{:S(2)}, u32[]{:S(2)}) collective-permute-start(f32[320,256]{1,0:T(8,128)S(1)} %maximum_add_fusion), channel_id=1, source_target_pairs={{0,0},{1,32},{2,2},{3,34},{4,4},{5,36},{6,6},{7,38},{8,8},{9,40},{... | collective-permute-start | bytes 983048 | tf_op jit(solution)/shard_map/ppermute | solution.py:31
  166.1 11.0 %collective-permute-start.30 = (f32[64,256]{1,0:T(8,128)S(1)}, f32[64,256]{1,0:T(8,128)S(1)}, u32[]{:S(2)}, u32[]{:S(2)}) collective-permute-start(f32[64,256]{1,0:T(8,128)S(1)} %fusion.234), channel_id=1, source_target_pairs={{0,64},{1,65},{2,66},{3,67},{4,68},{5,69},{6,70},{7,71},{8,72},{9,... | collective-permute-start | bytes 196616 | tf_op jit(solution)/shard_map/ppermute | solution.py:31
  189.6 4.1 %collective-permute-done.34 = f32[256,256]{1,0:T(8,128)S(1)} collective-permute-done((f32[256,256]{1,0:T(8,128)S(1)}, f32[256,256]{1,0:T(8,128)S(1)}, u32[]{:S(2)}, u32[]{:S(2)}) %collective-permute-start.34) | collective-permute-done | bytes 262176 | tf_op jit(solution)/shard_map/ppermute | solution.py:31
  193.7 6.3 %collective-permute-done.33 = f32[256,256]{1,0:T(8,128)S(1)} collective-permute-done((f32[256,256]{1,0:T(8,128)S(1)}, f32[256,256]{1,0:T(8,128)S(1)}, u32[]{:S(2)}, u32[]{:S(2)}) %collective-permute-start.33) | collective-permute-done | bytes 262176 | tf_op jit(solution)/shard_map/ppermute | solution.py:31
  205.8 3.4 collective-permute-start.36
  210.1 11.4 %collective-permute-done.36 = f32[64,256]{1,0:T(8,128)S(1)} collective-permute-done((f32[64,256]{1,0:T(8,128)S(1)}, f32[64,256]{1,0:T(8,128)S(1)}, u32[]{:S(2)}, u32[]{:S(2)}) %collective-permute-start.36) | collective-permute-done | bytes 65568 | tf_op jit(solution)/shard_map/ppermute | solution.py:31
  225.7 4.3 %collective-permute-start.40 = (f32[64,256]{1,0:T(8,128)S(1)}, f32[64,256]{1,0:T(8,128)S(1)}, u32[]{:S(2)}, u32[]{:S(2)}) collective-permute-start(f32[64,256]{1,0:T(8,128)S(1)} %fusion.228), channel_id=1, source_target_pairs={{0,4},{1,5},{2,68},{3,69},{4,132},{5,133},{6,196},{7,197},{8,12},{... | collective-permute-start | bytes 196616 | tf_op jit(solution)/shard_map/ppermute | solution.py:31
  231.3 6.4 %collective-permute-start.50 = (f32[64,256]{1,0:T(8,128)S(1)}, f32[64,256]{1,0:T(8,128)S(1)}, u32[]{:S(2)}, u32[]{:S(2)}) collective-permute-start(f32[64,256]{1,0:T(8,128)S(1)} %fusion.228), channel_id=1, source_target_pairs={{0,0},{1,32},{2,2},{3,34},{4,4},{5,36},{6,6},{7,38},{8,8},{9,40},{... | collective-permute-start | bytes 196616 | tf_op jit(solution)/shard_map/ppermute | solution.py:31
  238.1 4.1 %collective-permute-start.82 = (f32[320,256]{1,0:T(8,128)S(1)}, f32[320,256]{1,0:T(8,128)S(1)}, u32[]{:S(2)}, u32[]{:S(2)}) collective-permute-start(f32[320,256]{1,0:T(8,128)S(1)} %maximum_add_fusion.2), channel_id=1, source_target_pairs={{0,0},{1,32},{2,2},{3,34},{4,4},{5,36},{6,6},{7,38},{8,8},{9,40},{... | collective-permute-start | bytes 983048 | tf_op jit(solution)/shard_map/ppermute | solution.py:31
  253.5 4.8 %collective-permute-done.44 = f32[256,256]{1,0:T(8,128)S(1)} collective-permute-done((f32[256,256]{1,0:T(8,128)S(1)}, f32[256,256]{1,0:T(8,128)S(1)}, u32[]{:S(2)}, u32[]{:S(2)}) %collective-permute-start.44) | collective-permute-done | bytes 262176 | tf_op jit(solution)/shard_map/ppermute | solution.py:31
  263.3 11.0 %collective-permute-start.49 = (f32[64,256]{1,0:T(8,128)S(1)}, f32[64,256]{1,0:T(8,128)S(1)}, u32[]{:S(2)}, u32[]{:S(2)}) collective-permute-start(f32[64,256]{1,0:T(8,128)S(1)} %get-tuple-element.51), channel_id=1, source_target_pairs={{0,128},{1,129},{2,130},{3,131},{4,132},{5,133},{6,134},{7,135},{8... | collective-permute-start | bytes 196616 | tf_op jit(solution)/shard_map/ppermute | solution.py:31
  279.4 5.5 %collective-permute-start.56 = (f32[64,256]{1,0:T(8,128)S(1)}, f32[64,256]{1,0:T(8,128)S(1)}, u32[]{:S(2)}, u32[]{:S(2)}) collective-permute-start(f32[64,256]{1,0:T(8,128)S(1)} %fusion.232), channel_id=1, source_target_pairs={{0,6},{1,71},{2,70},{3,135},{4,134},{5,199},{6,198},{7,7},{8,14},{... | collective-permute-start | bytes 196616 | tf_op jit(solution)/shard_map/ppermute | solution.py:31
  284.9 4.4 %collective-permute-start.57 = (f32[64,256]{1,0:T(8,128)S(1)}, f32[64,256]{1,0:T(8,128)S(1)}, u32[]{:S(2)}, u32[]{:S(2)}) collective-permute-start(f32[64,256]{1,0:T(8,128)S(1)} %fusion.232), channel_id=1, source_target_pairs={{0,4},{1,69},{2,68},{3,133},{4,132},{5,197},{6,196},{7,5},{8,12},{... | collective-permute-start | bytes 196616 | tf_op jit(solution)/shard_map/ppermute | solution.py:31
  291.2 4.1 %collective-permute-start.59 = (f32[64,256]{1,0:T(8,128)S(1)}, f32[64,256]{1,0:T(8,128)S(1)}, u32[]{:S(2)}, u32[]{:S(2)}) collective-permute-start(f32[64,256]{1,0:T(8,128)S(1)} %fusion.232), channel_id=1, source_target_pairs={{0,0},{1,65},{2,64},{3,129},{4,128},{5,193},{6,192},{7,1},{8,8},{9... | collective-permute-start | bytes 196616 | tf_op jit(solution)/shard_map/ppermute | solution.py:31
  319.0 5.6 %collective-permute-start.66 = (f32[64,256]{1,0:T(8,128)S(1)}, f32[64,256]{1,0:T(8,128)S(1)}, u32[]{:S(2)}, u32[]{:S(2)}) collective-permute-start(f32[64,256]{1,0:T(8,128)S(1)} %get-tuple-element.44), channel_id=1, source_target_pairs={{0,128},{1,129},{2,130},{3,131},{4,132},{5,133},{6,134},{7,135},{8... | collective-permute-start | bytes 196616 | tf_op jit(solution)/shard_map/ppermute | solution.py:31
  329.7 6.0 %collective-permute-start.70 = (f32[64,256]{1,0:T(8,128)S(1)}, f32[64,256]{1,0:T(8,128)S(1)}, u32[]{:S(2)}, u32[]{:S(2)}) collective-permute-start(f32[64,256]{1,0:T(8,128)S(1)} %fusion.236), channel_id=1, source_target_pairs={{0,6},{1,71},{2,70},{3,135},{4,134},{5,199},{6,198},{7,7},{8,14},{... | collective-permute-start | bytes 196616 | tf_op jit(solution)/shard_map/ppermute | solution.py:31
  345.8 5.7 %collective-permute-start.81 = (f32[64,256]{1,0:T(8,128)S(1)}, f32[64,256]{1,0:T(8,128)S(1)}, u32[]{:S(2)}, u32[]{:S(2)}) collective-permute-start(f32[64,256]{1,0:T(8,128)S(1)} %fusion.236), channel_id=1, source_target_pairs={{0,0},{1,34},{2,2},{3,36},{4,4},{5,38},{6,6},{7,32},{8,8},{9,42},{... | collective-permute-start | bytes 196616 | tf_op jit(solution)/shard_map/ppermute | solution.py:31
  355.3 5.5 %collective-permute-done.76 = f32[256,256]{1,0:T(8,128)S(1)} collective-permute-done((f32[256,256]{1,0:T(8,128)S(1)}, f32[256,256]{1,0:T(8,128)S(1)}, u32[]{:S(2)}, u32[]{:S(2)}) %collective-permute-start.76) | collective-permute-done | bytes 262176 | tf_op jit(solution)/shard_map/ppermute | solution.py:31
  362.5 4.4 %collective-permute-done.75 = f32[256,256]{1,0:T(8,128)S(1)} collective-permute-done((f32[256,256]{1,0:T(8,128)S(1)}, f32[256,256]{1,0:T(8,128)S(1)}, u32[]{:S(2)}, u32[]{:S(2)}) %collective-permute-start.75) | collective-permute-done | bytes 262176 | tf_op jit(solution)/shard_map/ppermute | solution.py:31
  374.3 4.8 %collective-permute-start.80 = (f32[64,256]{1,0:T(8,128)S(1)}, f32[64,256]{1,0:T(8,128)S(1)}, u32[]{:S(2)}, u32[]{:S(2)}) collective-permute-start(f32[64,256]{1,0:T(8,128)S(1)} %get-tuple-element.37), channel_id=1, source_target_pairs={{0,128},{1,129},{2,130},{3,131},{4,132},{5,133},{6,134},{7,135},{8... | collective-permute-start | bytes 196616 | tf_op jit(solution)/shard_map/ppermute | solution.py:31
  (319 shorter events, 178.3 us)
Async XLA Ops:
  2.9 29.5 %collective-permute-start.7 = (f32[4,256,256]{2,1,0:T(8,128)S(1)}, f32[4,256,256]{2,1,0:T(8,128)}, u32[]{:S(2)}, u32[]{:S(2)}) collective-permute-start(f32[4,256,256]{2,1,0:T(8,128)S(1)} %bitcast_multiply_fusion), channel_id=1, source_target_pairs={{0,7},{1,2},{2,1},{3,4},{4,3},{5,6},{6,5},{7,0},{8,15},{9,10},{10,... | collective-permute-start | bytes 3145736 | tf_op jit(solution)/shard_map/ppermute | solution.py:31
  10.8 23.9 %collective-permute-start.2 = (f32[4,256,256]{2,1,0:T(8,128)S(1)}, f32[4,256,256]{2,1,0:T(8,128)}, u32[]{:S(2)}, u32[]{:S(2)}) collective-permute-start(f32[4,256,256]{2,1,0:T(8,128)S(1)} %fusion.63), channel_id=1, source_target_pairs={{0,1},{1,0},{2,3},{3,2},{4,5},{5,4},{6,7},{7,6},{8,9},{9,8},{10,11... | collective-permute-start | bytes 3145736 | tf_op jit(solution)/shard_map/ppermute | solution.py:31
  13.4 26.8 %collective-permute-start.1 = (f32[256,256]{1,0:T(8,128)}, f32[256,256]{1,0:T(8,128)S(1)}, u32[]{:S(2)}, u32[]{:S(2)}) collective-permute-start(f32[256,256]{1,0:T(8,128)} %bitcast.11), channel_id=1, source_target_pairs={{0,1},{1,0},{2,3},{3,2},{4,5},{5,4},{6,7},{7,6},{8,9},{9,8},{10,11... | collective-permute-start | bytes 786440 | tf_op jit(solution)/shard_map/ppermute | solution.py:31
  38.5 22.2 %collective-permute-start.6 = (f32[4,256,256]{2,1,0:T(8,128)S(1)}, f32[4,256,256]{2,1,0:T(8,128)S(1)}, u32[]{:S(2)}, u32[]{:S(2)}) collective-permute-start(f32[4,256,256]{2,1,0:T(8,128)S(1)} %get-tuple-element.15), channel_id=1, source_target_pairs={{0,1},{1,0},{2,3},{3,2},{4,5},{5,4},{6,7},{7,6},{8,9},{9,8},{10,11... | collective-permute-start | bytes 3145736 | tf_op jit(solution)/shard_map/ppermute | solution.py:31
  41.5 29.5 %collective-permute-start.5 = (f32[256,256]{1,0:T(8,128)S(1)}, f32[256,256]{1,0:T(8,128)S(1)}, u32[]{:S(2)}, u32[]{:S(2)}) collective-permute-start(f32[256,256]{1,0:T(8,128)S(1)} %convolution_add_fusion.28), channel_id=1, source_target_pairs={{0,16},{1,17},{2,18},{3,19},{4,20},{5,21},{6,22},{7,23},{8,24},{9,... | collective-permute-start | bytes 786440 | tf_op jit(solution)/shard_map/ppermute | solution.py:31
  45.8 25.2 %collective-permute-start.4 = (f32[256,256]{1,0:T(8,128)S(1)}, f32[256,256]{1,0:T(8,128)S(1)}, u32[]{:S(2)}, u32[]{:S(2)}) collective-permute-start(f32[256,256]{1,0:T(8,128)S(1)} %convolution_add_fusion.29), channel_id=1, source_target_pairs={{0,24},{1,25},{2,26},{3,27},{4,28},{5,29},{6,30},{7,31},{8,16},{9,... | collective-permute-start | bytes 786440 | tf_op jit(solution)/shard_map/ppermute | solution.py:31
  46.7 23.1 %collective-permute-start.8 = (f32[4,256,256]{2,1,0:T(8,128)S(1)}, f32[4,256,256]{2,1,0:T(8,128)S(1)}, u32[]{:S(2)}, u32[]{:S(2)}) collective-permute-start(f32[4,256,256]{2,1,0:T(8,128)S(1)} %get-tuple-element.14), channel_id=1, source_target_pairs={{0,7},{1,2},{2,1},{3,4},{4,3},{5,6},{6,5},{7,0},{8,15},{9,10},{10,... | collective-permute-start | bytes 3145736 | tf_op jit(solution)/shard_map/ppermute | solution.py:31
  48.3 22.7 %collective-permute-start.3 = (f32[256,256]{1,0:T(8,128)S(1)}, f32[256,256]{1,0:T(8,128)S(1)}, u32[]{:S(2)}, u32[]{:S(2)}) collective-permute-start(f32[256,256]{1,0:T(8,128)S(1)} %convolution_add_fusion.30), channel_id=1, source_target_pairs={{0,8},{1,9},{2,10},{3,11},{4,12},{5,13},{6,14},{7,15},{8,0},{9,1},... | collective-permute-start | bytes 786440 | tf_op jit(solution)/shard_map/ppermute | solution.py:31
  60.6 29.2 %collective-permute-start = (f32[320,256]{1,0:T(8,128)S(1)}, f32[320,256]{1,0:T(8,128)S(1)}, u32[]{:S(2)}, u32[]{:S(2)}) collective-permute-start(f32[320,256]{1,0:T(8,128)S(1)} %copy-done.3), channel_id=1, source_target_pairs={{0,0},{1,34},{2,2},{3,36},{4,4},{5,38},{6,6},{7,32},{8,8},{9,42},{... | collective-permute-start | bytes 983048 | tf_op jit(solution)/shard_map/ppermute | solution.py:31
  72.3 16.4 %collective-permute-start.12 = (f32[64,256]{1,0:T(8,128)S(1)}, f32[64,256]{1,0:T(8,128)S(1)}, u32[]{:S(2)}, u32[]{:S(2)}) collective-permute-start(f32[64,256]{1,0:T(8,128)S(1)} %get-tuple-element.78), channel_id=1, source_target_pairs={{0,192},{1,199},{2,128},{3,135},{4,64},{5,71},{6,0},{7,7},{8,200},... | collective-permute-start | bytes 196616 | tf_op jit(solution)/shard_map/ppermute | solution.py:31
  98.6 43.8 %collective-permute-start.18 = (f32[4,256,256]{2,1,0:T(8,128)S(1)}, f32[4,256,256]{2,1,0:T(8,128)S(1)}, u32[]{:S(2)}, u32[]{:S(2)}) collective-permute-start(f32[4,256,256]{2,1,0:T(8,128)S(1)} %get-tuple-element.12), channel_id=1, source_target_pairs={{0,1},{1,0},{2,3},{3,2},{4,5},{5,4},{6,7},{7,6},{8,9},{9,8},{10,11... | collective-permute-start | bytes 3145736 | tf_op jit(solution)/shard_map/ppermute | solution.py:31
  110.5 26.1 %collective-permute-start.23 = (f32[4,256,256]{2,1,0:T(8,128)S(1)}, f32[4,256,256]{2,1,0:T(8,128)S(1)}, u32[]{:S(2)}, u32[]{:S(2)}) collective-permute-start(f32[4,256,256]{2,1,0:T(8,128)S(1)} %get-tuple-element.13), channel_id=1, source_target_pairs={{0,7},{1,2},{2,1},{3,4},{4,3},{5,6},{6,5},{7,0},{8,15},{9,10},{10,... | collective-permute-start | bytes 3145736 | tf_op jit(solution)/shard_map/ppermute | solution.py:31
  114.8 28.8 %collective-permute-start.22 = (f32[256,256]{1,0:T(8,128)S(1)}, f32[256,256]{1,0:T(8,128)S(1)}, u32[]{:S(2)}, u32[]{:S(2)}) collective-permute-start(f32[256,256]{1,0:T(8,128)S(1)} %fusion.12), channel_id=1, source_target_pairs={{0,16},{1,17},{2,18},{3,19},{4,20},{5,21},{6,22},{7,23},{8,24},{9,... | collective-permute-start | bytes 786440 | tf_op jit(solution)/shard_map/ppermute | solution.py:31
  116.6 27.0 %collective-permute-start.21 = (f32[256,256]{1,0:T(8,128)S(1)}, f32[256,256]{1,0:T(8,128)S(1)}, u32[]{:S(2)}, u32[]{:S(2)}) collective-permute-start(f32[256,256]{1,0:T(8,128)S(1)} %fusion.13), channel_id=1, source_target_pairs={{0,24},{1,25},{2,26},{3,27},{4,28},{5,29},{6,30},{7,31},{8,16},{9,... | collective-permute-start | bytes 786440 | tf_op jit(solution)/shard_map/ppermute | solution.py:31
  119.7 24.0 %collective-permute-start.20 = (f32[256,256]{1,0:T(8,128)S(1)}, f32[256,256]{1,0:T(8,128)S(1)}, u32[]{:S(2)}, u32[]{:S(2)}) collective-permute-start(f32[256,256]{1,0:T(8,128)S(1)} %fusion.14), channel_id=1, source_target_pairs={{0,8},{1,9},{2,10},{3,11},{4,12},{5,13},{6,14},{7,15},{8,0},{9,1},... | collective-permute-start | bytes 786440 | tf_op jit(solution)/shard_map/ppermute | solution.py:31
  136.6 21.4 %collective-permute-start.19 = (f32[320,256]{1,0:T(8,128)S(1)}, f32[320,256]{1,0:T(8,128)S(1)}, u32[]{:S(2)}, u32[]{:S(2)}) collective-permute-start(f32[320,256]{1,0:T(8,128)S(1)} %maximum_add_fusion.1), channel_id=1, source_target_pairs={{0,0},{1,34},{2,2},{3,36},{4,4},{5,38},{6,6},{7,32},{8,8},{9,42},{... | collective-permute-start | bytes 983048 | tf_op jit(solution)/shard_map/ppermute | solution.py:31
  144.1 20.6 %collective-permute-start.27 = (f32[64,256]{1,0:T(8,128)S(1)}, f32[64,256]{1,0:T(8,128)S(1)}, u32[]{:S(2)}, u32[]{:S(2)}) collective-permute-start(f32[64,256]{1,0:T(8,128)S(1)} %get-tuple-element.70), channel_id=1, source_target_pairs={{0,192},{1,199},{2,128},{3,135},{4,64},{5,71},{6,0},{7,7},{8,200},... | collective-permute-start | bytes 196616 | tf_op jit(solution)/shard_map/ppermute | solution.py:31
  146.7 18.0 %collective-permute-start.26 = (f32[64,256]{1,0:T(8,128)S(1)}, f32[64,256]{1,0:T(8,128)S(1)}, u32[]{:S(2)}, u32[]{:S(2)}) collective-permute-start(f32[64,256]{1,0:T(8,128)S(1)} %get-tuple-element.71), channel_id=1, source_target_pairs={{0,128},{1,135},{2,192},{3,199},{4,0},{5,7},{6,64},{7,71},{8,136},... | collective-permute-start | bytes 196616 | tf_op jit(solution)/shard_map/ppermute | solution.py:31
  148.5 16.2 %collective-permute-start.24 = (f32[64,256]{1,0:T(8,128)S(1)}, f32[64,256]{1,0:T(8,128)S(1)}, u32[]{:S(2)}, u32[]{:S(2)}) collective-permute-start(f32[64,256]{1,0:T(8,128)S(1)} %get-tuple-element.72), channel_id=1, source_target_pairs={{0,0},{1,7},{2,64},{3,71},{4,128},{5,135},{6,192},{7,199},{8,8},{9... | collective-permute-start | bytes 196616 | tf_op jit(solution)/shard_map/ppermute | solution.py:31
  150.7 14.0 %collective-permute-start.25 = (f32[64,256]{1,0:T(8,128)S(1)}, f32[64,256]{1,0:T(8,128)S(1)}, u32[]{:S(2)}, u32[]{:S(2)}) collective-permute-start(f32[64,256]{1,0:T(8,128)S(1)} %get-tuple-element.69), channel_id=1, source_target_pairs={{0,64},{1,71},{2,0},{3,7},{4,192},{5,199},{6,128},{7,135},{8,72},{... | collective-permute-start | bytes 196616 | tf_op jit(solution)/shard_map/ppermute | solution.py:31
  158.0 51.3 %collective-permute-start.17 = (f32[320,256]{1,0:T(8,128)S(1)}, f32[320,256]{1,0:T(8,128)S(1)}, u32[]{:S(2)}, u32[]{:S(2)}) collective-permute-start(f32[320,256]{1,0:T(8,128)S(1)} %maximum_add_fusion), channel_id=1, source_target_pairs={{0,0},{1,32},{2,2},{3,34},{4,4},{5,36},{6,6},{7,38},{8,8},{9,40},{... | collective-permute-start | bytes 983048 | tf_op jit(solution)/shard_map/ppermute | solution.py:31
  185.3 14.6 %collective-permute-start.33 = (f32[256,256]{1,0:T(8,128)S(1)}, f32[256,256]{1,0:T(8,128)S(1)}, u32[]{:S(2)}, u32[]{:S(2)}) collective-permute-start(f32[256,256]{1,0:T(8,128)S(1)} %fusion.35), channel_id=1, source_target_pairs={{0,24},{1,25},{2,26},{3,27},{4,28},{5,29},{6,30},{7,31},{8,16},{9,... | collective-permute-start | bytes 786440 | tf_op jit(solution)/shard_map/ppermute | solution.py:31
  205.8 15.6 %collective-permute-start.36 = (f32[64,256]{1,0:T(8,128)S(1)}, f32[64,256]{1,0:T(8,128)S(1)}, u32[]{:S(2)}, u32[]{:S(2)}) collective-permute-start(f32[64,256]{1,0:T(8,128)S(1)} %get-tuple-element.61), channel_id=1, source_target_pairs={{0,64},{1,65},{2,0},{3,1},{4,192},{5,193},{6,128},{7,129},{8,72},{... | collective-permute-start | bytes 196616 | tf_op jit(solution)/shard_map/ppermute | solution.py:31
  231.3 14.7 %collective-permute-start.50 = (f32[64,256]{1,0:T(8,128)S(1)}, f32[64,256]{1,0:T(8,128)S(1)}, u32[]{:S(2)}, u32[]{:S(2)}) collective-permute-start(f32[64,256]{1,0:T(8,128)S(1)} %fusion.228), channel_id=1, source_target_pairs={{0,0},{1,32},{2,2},{3,34},{4,4},{5,36},{6,6},{7,38},{8,8},{9,40},{... | collective-permute-start | bytes 196616 | tf_op jit(solution)/shard_map/ppermute | solution.py:31
  238.1 141.0 %collective-permute-start.82 = (f32[320,256]{1,0:T(8,128)S(1)}, f32[320,256]{1,0:T(8,128)S(1)}, u32[]{:S(2)}, u32[]{:S(2)}) collective-permute-start(f32[320,256]{1,0:T(8,128)S(1)} %maximum_add_fusion.2), channel_id=1, source_target_pairs={{0,0},{1,32},{2,2},{3,34},{4,4},{5,36},{6,6},{7,38},{8,8},{9,40},{... | collective-permute-start | bytes 983048 | tf_op jit(solution)/shard_map/ppermute | solution.py:31
  248.8 25.5 %collective-permute-start.55 = (f32[256,256]{1,0:T(8,128)S(1)}, f32[256,256]{1,0:T(8,128)S(1)}, u32[]{:S(2)}, u32[]{:S(2)}) collective-permute-start(f32[256,256]{1,0:T(8,128)S(1)} %select_add_fusion.2), channel_id=1, source_target_pairs={{0,1},{1,0},{2,3},{3,2},{4,5},{5,4},{6,7},{7,6},{8,9},{9,8},{10,11... | collective-permute-start | bytes 786440 | tf_op jit(solution)/shard_map/ppermute | solution.py:31
  279.4 16.6 %collective-permute-start.56 = (f32[64,256]{1,0:T(8,128)S(1)}, f32[64,256]{1,0:T(8,128)S(1)}, u32[]{:S(2)}, u32[]{:S(2)}) collective-permute-start(f32[64,256]{1,0:T(8,128)S(1)} %fusion.232), channel_id=1, source_target_pairs={{0,6},{1,71},{2,70},{3,135},{4,134},{5,199},{6,198},{7,7},{8,14},{... | collective-permute-start | bytes 196616 | tf_op jit(solution)/shard_map/ppermute | solution.py:31
  329.7 16.1 %collective-permute-start.70 = (f32[64,256]{1,0:T(8,128)S(1)}, f32[64,256]{1,0:T(8,128)S(1)}, u32[]{:S(2)}, u32[]{:S(2)}) collective-permute-start(f32[64,256]{1,0:T(8,128)S(1)} %fusion.236), channel_id=1, source_target_pairs={{0,6},{1,71},{2,70},{3,135},{4,134},{5,199},{6,198},{7,7},{8,14},{... | collective-permute-start | bytes 196616 | tf_op jit(solution)/shard_map/ppermute | solution.py:31
  335.6 15.8 %collective-permute-start.71 = (f32[64,256]{1,0:T(8,128)S(1)}, f32[64,256]{1,0:T(8,128)S(1)}, u32[]{:S(2)}, u32[]{:S(2)}) collective-permute-start(f32[64,256]{1,0:T(8,128)S(1)} %fusion.236), channel_id=1, source_target_pairs={{0,4},{1,69},{2,68},{3,133},{4,132},{5,197},{6,196},{7,5},{8,12},{... | collective-permute-start | bytes 196616 | tf_op jit(solution)/shard_map/ppermute | solution.py:31
  345.8 26.1 %collective-permute-start.81 = (f32[64,256]{1,0:T(8,128)S(1)}, f32[64,256]{1,0:T(8,128)S(1)}, u32[]{:S(2)}, u32[]{:S(2)}) collective-permute-start(f32[64,256]{1,0:T(8,128)S(1)} %fusion.236), channel_id=1, source_target_pairs={{0,0},{1,34},{2,2},{3,36},{4,4},{5,38},{6,6},{7,32},{8,8},{9,42},{... | collective-permute-start | bytes 196616 | tf_op jit(solution)/shard_map/ppermute | solution.py:31
  351.5 21.5 %collective-permute-start.69 = (f32[256,256]{1,0:T(8,128)S(1)}, f32[256,256]{1,0:T(8,128)S(1)}, u32[]{:S(2)}, u32[]{:S(2)}) collective-permute-start(f32[256,256]{1,0:T(8,128)S(1)} %broadcast_add_fusion), channel_id=1, source_target_pairs={{0,7},{1,2},{2,1},{3,4},{4,3},{5,6},{6,5},{7,0},{8,15},{9,10},{10,... | collective-permute-start | bytes 786440 | tf_op jit(solution)/shard_map/ppermute | solution.py:31
  351.9 15.0 %collective-permute-start.75 = (f32[256,256]{1,0:T(8,128)S(1)}, f32[256,256]{1,0:T(8,128)S(1)}, u32[]{:S(2)}, u32[]{:S(2)}) collective-permute-start(f32[256,256]{1,0:T(8,128)S(1)} %pad_maximum_fusion.9), channel_id=1, source_target_pairs={{0,24},{1,25},{2,26},{3,27},{4,28},{5,29},{6,30},{7,31},{8,16},{9,... | collective-permute-start | bytes 786440 | tf_op jit(solution)/shard_map/ppermute | solution.py:31
  (56 other events, 511.4 us)
